TPU v7x, 32 devices: a whole 2x2x4 slice. The times are simulated.
32 devices in a mesh: tx: 8 (over y, x, core), ty: 4 (over z).
Axes of the slice: x: 2, y: 2, z: 4, core: 2. Of those that a mesh axis runs over, the one named last changes fastest.
Arguments:
- adjoint_in: float32 [5, 3, 64, 64, 128], P(None, None, 'ty', 'tx'), may hold values from -6 to 6
- courant: float32 [2, 3, 64, 64, 128], P(None, None, 'ty', 'tx'), may hold values from -0.45 to 0.45
- vertical_inverse: float32 [5, 128, 128], replicated, as said below
- links: int32 [40, 4], replicated, may hold values from 0 to 95, as said below
Outputs:
- adjoint_out: float32 [5, 3, 64, 64, 128], P(None, None, 'ty', 'tx')
Inputs may be any that keep to these rules, and one draw needn't show every extreme that they name: `links`: the three panel slots hold three faces of a cube that meet at one corner, in an order drawn afresh; call them X, Y, Z. X's east side joins Y's west side (code 0, both ways, tile row to same tile row), X's north side joins Z's south side (code 1, both ways, tile column to same tile column), Y's north side joins Z's east side with rotation: cell x = i of Y's top row is the neighbour of cell y = i of Z's east column (code 2 for Z's east ghosts, two rows a tile with off 0 and 8; code 3 for Y's north ghosts, one row a tile with off 0 or 8); all other panel sides are open. Row order is drawn afresh. Offsets are 0 or 8, codes 0 to 3. `vertical_inverse`: each block has a diagonal in [0.6, 1.0) and independent off-diagonal entries.
All inputs are finite; a program needn't handle non-finite values.
Results may differ from a plain program's by a relative error of at most 0.0003.
Values sent between devices are 32-bit elements; how exact they have to be, the bound alone decides.
A program may use at most 64 MiB of HBM per device.

v0:
```python
import jax
import jax.numpy as jnp
from jax import lax
from jax.sharding import PartitionSpec as P

STEPS = 2


def with_halo(block, sides, width):
    for axis, dim in sides:
        count = lax.axis_size(axis)
        forward = [(i, i + 1) for i in range(count - 1)]
        forward.append((count - 1, 0))
        backward = [(target, source) for source, target in forward]
        low = lax.ppermute(
            lax.slice_in_dim(block, block.shape[dim] - width, None, axis=dim), axis, forward
        )
        high = lax.ppermute(lax.slice_in_dim(block, 0, width, axis=dim), axis, backward)
        block = jnp.concatenate([low, block, high], axis=dim)
    return block


def broadcast(block, axis, source):
    block = jnp.where(lax.axis_index(axis) == source, block, jnp.zeros_like(block))
    return lax.psum(block, axis)


def link_tables(links, own_tile, tile_count, slot_count):
    source_slot = links[:, 0] // tile_count
    target_slot = links[:, 1] // tile_count
    target_tile = links[:, 1] % tile_count
    offset = links[:, 2]
    link_kind = links[:, 3]
    slot_ids = jnp.arange(slot_count, dtype=jnp.int32)
    target_hot = (target_slot[:, None] == slot_ids[None, :]).astype(jnp.float32)
    source_hot = (source_slot[:, None] == slot_ids[None, :]).astype(jnp.float32)

    def slot_table(wanted):
        chosen = (
            (target_tile == own_tile) & (link_kind == wanted) & ((link_kind != 2) | (offset == 0))
        )
        weight = chosen.astype(jnp.float32)
        return jnp.sum(
            weight[:, None, None] * target_hot[:, :, None] * source_hot[:, None, :], axis=0
        )

    north_source = jnp.max(jnp.where(link_kind == 2, source_slot, 0))
    east_source = jnp.max(jnp.where(link_kind == 3, source_slot, 0))
    return (slot_table(0), slot_table(1), slot_table(2), slot_table(3), north_source, east_source)


def mix_slots(slot_table, pieces):
    return jnp.sum(slot_table[None, :, :, None, None] * pieces[:, None], axis=2)


def on_device(adjoint_in, courant, vertical_inverse, links):
    col_count = lax.axis_size("tx")
    row_count = lax.axis_size("ty")
    column = lax.axis_index("tx")
    row_index = lax.axis_index("ty")
    slot_count = adjoint_in.shape[1]
    cells_y = adjoint_in.shape[2]
    cells_x = adjoint_in.shape[3]
    tile_count = col_count * row_count
    own_tile = row_index * col_count + column
    x_table, y_table, east_table, north_table, north_source, east_source = link_tables(
        links, own_tile, tile_count, slot_count
    )
    at_east = column == col_count - 1
    at_west = column == 0
    at_north = row_index == row_count - 1
    at_south = row_index == 0
    adjoint = adjoint_in
    for step_index in range(STEPS):
        mixed = jnp.einsum(
            "slm,skyxl->skyxm", vertical_inverse, adjoint, precision=lax.Precision.HIGHEST
        )
        fluxes = courant[:, None] * mixed[None]
        padded = with_halo(fluxes, (("tx", 4), ("ty", 3)), 1)
        halo_east = padded[0, :, :, 1:-1, cells_x + 1]
        halo_west = padded[0, :, :, 1:-1, 0]
        halo_north = padded[1, :, :, cells_y + 1, 1:-1]
        halo_south = padded[1, :, :, 0, 1:-1]
        top_rows = lax.dynamic_slice_in_dim(fluxes[1, :, :, cells_y - 1], north_source, 1, 1)
        east_cols = lax.dynamic_slice_in_dim(fluxes[0, :, :, :, cells_x - 1], east_source, 1, 1)
        north_below = broadcast(top_rows, "ty", row_count - 1)
        north_whole = lax.all_gather(north_below, "tx", axis=2, tiled=True)
        east_beside = broadcast(east_cols, "tx", col_count - 1)
        east_whole = lax.all_gather(east_beside, "ty", axis=2, tiled=True)
        north_piece = lax.dynamic_slice_in_dim(north_whole, row_index * cells_y, cells_y, 2)
        east_piece = lax.dynamic_slice_in_dim(east_whole, column * cells_x, cells_x, 2)
        rotated_east = -jnp.sum(east_table, axis=1)[None, :, None, None] * north_piece
        rotated_north = -jnp.sum(north_table, axis=1)[None, :, None, None] * east_piece
        ghost_east = jnp.where(at_east, mix_slots(x_table, halo_east) + rotated_east, halo_east)
        ghost_west = jnp.where(at_west, mix_slots(x_table, halo_west), halo_west)
        ghost_north = jnp.where(
            at_north, mix_slots(y_table, halo_north) + rotated_north, halo_north
        )
        ghost_south = jnp.where(at_south, mix_slots(y_table, halo_south), halo_south)
        x_line = jnp.concatenate(
            [ghost_west[:, :, :, None], fluxes[0], ghost_east[:, :, :, None]], axis=3
        )
        y_line = jnp.concatenate(
            [ghost_south[:, :, None], fluxes[1], ghost_north[:, :, None]], axis=2
        )
        adjoint = (
            mixed
            + 0.5 * (x_line[:, :, :, 2:] - x_line[:, :, :, :-2])
            + 0.5 * (y_line[:, :, 2:] - y_line[:, :, :-2])
        )
    return adjoint


def solution(mesh):
    placed = (P(None, None, "ty", "tx", None), P(None, None, "ty", "tx", None), P(), P())
    return jax.shard_map(
        on_device,
        mesh=mesh,
        in_specs=placed,
        out_specs=P(None, None, "ty", "tx", None),
        check_vma=False,
    )
```

profile of v0, /device:TPU:0, one launch (start us, length us, event | category | flops | bytes accessed | tf_op | source)
XLA Modules:
  0.0 178.6 jit_solution(6658720027340490278)
XLA Ops:
  0.0 1.2 copy.186
  1.2 0.2 copy-done
  1.3 1.9 %fusion.13 = f32[5,3,16,8,128]{4,3,2,1,0:T(8,128)S(1)} fusion(f32[5,3,16,8,128]{4,3,2,1,0:T(8,128)S(1)} %copy-done, f32[5,128,128]{2,1,0:T(8,128)} %param.6), kind=kOutput, calls=%fused_computation.33 | convolution fusion | flops 377487360 | bytes 2293760 | tf_op jit(solution)/shard_map/slm,skyxl->skyxm/dot_general | solution.py:75
  3.3 0.0 copy-start.1
  3.3 0.9 copy-done.1
  4.2 0.2 copy.187
  4.4 0.0 copy-start.8
  4.4 0.2 broadcast_multiply_fusion.1
  4.6 0.8 fusion.36
  5.4 0.5 collective-permute-start.1
  5.9 2.9 %collective-permute-start = (f32[2,5,3,16,1,128]{5,3,2,1,4,0:T(8,128)}, f32[2,5,3,16,1,128]{5,3,2,1,4,0:T(8,128)}, u32[]{:S(2)}, u32[]{:S(2)}) collective-permute-start(f32[2,5,3,16,1,128]{5,3,2,1,4,0:T(8,128)} %get-tuple-element.33), channel_id=1, source_target_pairs={{4,0},{8,4},{12,8},{16,12},{20,16},{24,20},{28,24},{0,28},{5,1},{9... | collective-permute-start | bytes 737288 | tf_op jit(solution)/shard_map/ppermute | solution.py:18
  8.8 0.7 fusion.28
  12.2 0.1 slice.156
  12.4 0.1 multiply_reduce_fusion.10
  12.5 0.6 neg.18
  13.1 0.5 neg.19
  14.3 20.5 %psum.28 = f32[5,1,8,128]{3,2,0,1:T(8,128)} all-reduce(f32[5,1,8,128]{3,2,0,1:T(8,128)S(1)} %bitcast.157), channel_id=1, replica_groups=mesh['tx'=8,'ty'=4] {'ty'}, use_global_device_ids=true, to_apply=%region_4.5 | all-reduce | flops 5120 | bytes 40960 | tf_op jit(solution)/shard_map/psum | solution.py:25
  35.5 22.7 %psum.29 = f32[5,1,16,128]{3,2,0,1:T(8,128)S(1)} all-reduce(f32[5,1,16,128]{3,2,0,1:T(8,128)S(1)} %select_bitcast_fusion.1), channel_id=1, replica_groups=mesh['tx'=8,'ty'=4] {'tx'}, use_global_device_ids=true, to_apply=%region_10.11 | all-reduce | flops 10240 | bytes 81920 | tf_op jit(solution)/shard_map/psum | solution.py:25
  58.3 13.5 %all_gather.13 = f32[5,1,64,128]{3,2,0,1:T(8,128)S(1)} all-gather(f32[5,1,16,128]{3,2,0,1:T(8,128)S(1)} %psum.29), channel_id=1, replica_groups=mesh['tx'=8,'ty'=4] {'ty'}, dimensions={2}, use_global_device_ids=true | all-gather | bytes 204800 | tf_op jit(solution)/shard_map/all_gather | solution.py:89
  71.7 9.5 %all_gather.12 = f32[5,1,64,128]{3,2,0,1:T(8,128)S(1)} all-gather(f32[5,1,8,128]{3,2,0,1:T(8,128)} %psum.28), channel_id=1, replica_groups=mesh['tx'=8,'ty'=4] {'tx'}, dimensions={2}, use_global_device_ids=true | all-gather | bytes 184320 | tf_op jit(solution)/shard_map/all_gather | solution.py:87
  81.2 0.1 slice_bitcast_fusion.2
  81.4 1.3 pad_maximum_fusion.13
  82.7 0.1 collective-permute-start.2
  82.8 1.9 %collective-permute-start.3 = (f32[2,5,3,1,10,128]{5,3,2,1,4,0:T(1,128)S(1)}, f32[2,5,3,1,10,128]{5,3,2,1,4,0:T(1,128)S(1)}, u32[]{:S(2)}, u32[]{:S(2)}) collective-permute-start(f32[2,5,3,1,10,128]{5,3,2,1,4,0:T(1,128)S(1)} %get-tuple-element.25), channel_id=1, source_target_pairs={{0,1},{1,2},{2,3},{3,0},{4,5},{5,6},{6,7},{7,4},{8,9},{9,10},{10,1... | collective-permute-start | bytes 460808 | tf_op jit(solution)/shard_map/ppermute | solution.py:15
  84.8 0.9 slice_bitcast_fusion.4
  85.7 0.9 slice_bitcast_fusion.5
  86.6 0.1 multiply_reduce_fusion.3
  86.7 1.0 bitcast_select_fusion.2
  87.7 0.9 bitcast_select_fusion.1
  88.6 0.1 fusion.7
  88.7 0.0 copy-start.2
  88.8 0.0 copy-start.7
  88.8 0.7 collective-permute-done.2
  89.5 2.8 %collective-permute-done.3 = f32[2,5,3,1,10,128]{5,3,2,1,4,0:T(1,128)S(1)} collective-permute-done((f32[2,5,3,1,10,128]{5,3,2,1,4,0:T(1,128)S(1)}, f32[2,5,3,1,10,128]{5,3,2,1,4,0:T(1,128)S(1)}, u32[]{:S(2)}, u32[]{:S(2)}) %collective-permute-start.3) | collective-permute-done | bytes 153632 | tf_op jit(solution)/shard_map/ppermute | solution.py:15
  92.4 0.1 multiply_reduce_fusion.7
  92.5 0.1 broadcast_select_fusion.2
  92.6 0.2 broadcast_select_fusion.4
  92.7 0.3 fusion.5
  93.0 1.7 fusion.9
  94.8 0.2 copy.201
  95.0 0.2 broadcast_multiply_fusion
  95.1 0.6 copy-done.3
  95.7 0.1 slice.166
  95.8 0.8 fusion.35
  96.6 1.4 slice_bitcast_fusion
  98.1 23.2 %psum.31 = f32[5,1,16,128]{3,2,0,1:T(8,128)S(1)} all-reduce(f32[5,1,16,128]{3,2,0,1:T(8,128)S(1)} %select_bitcast_fusion), channel_id=1, replica_groups=mesh['tx'=8,'ty'=4] {'tx'}, use_global_device_ids=true, to_apply=%region_16.17 | all-reduce | flops 10240 | bytes 81920 | tf_op jit(solution)/shard_map/psum | solution.py:25
  121.3 13.4 %all_gather.15 = f32[5,1,64,128]{3,2,0,1:T(8,128)S(1)} all-gather(f32[5,1,16,128]{3,2,0,1:T(8,128)S(1)} %psum.31), channel_id=1, replica_groups=mesh['tx'=8,'ty'=4] {'ty'}, dimensions={2}, use_global_device_ids=true | all-gather | bytes 204800 | tf_op jit(solution)/shard_map/all_gather | solution.py:89
  134.7 2.6 %collective-permute-start.4 = (f32[2,5,3,16,1,128]{5,3,2,1,4,0:T(8,128)}, f32[2,5,3,16,1,128]{5,3,2,1,4,0:T(8,128)S(1)}, u32[]{:S(2)}, u32[]{:S(2)}) collective-permute-start(f32[2,5,3,16,1,128]{5,3,2,1,4,0:T(8,128)} %get-tuple-element.29), channel_id=1, source_target_pairs={{4,0},{8,4},{12,8},{16,12},{20,16},{24,20},{28,24},{0,28},{5,1},{9... | collective-permute-start | bytes 737288 | tf_op jit(solution)/shard_map/ppermute | solution.py:18
  137.4 2.5 %copy.252 = f32[1,5,3,16,8,128]{5,4,3,2,1,0:T(8,128)} copy(f32[1,5,3,16,8,128]{5,3,2,1,4,0:T(8,128)} %get-tuple-element.27) | data formatting | bytes 1966080 | tf_op jit(solution)/shard_map/slice | solution.py:101
  139.9 17.6 %psum.30 = f32[5,1,8,128]{3,2,0,1:T(8,128)S(1)} all-reduce(f32[5,1,8,128]{3,2,0,1:T(8,128)S(1)} %bitcast.156), channel_id=1, replica_groups=mesh['tx'=8,'ty'=4] {'ty'}, use_global_device_ids=true, to_apply=%region_13.14 | all-reduce | flops 5120 | bytes 40960 | tf_op jit(solution)/shard_map/psum | solution.py:25
  157.5 8.7 %all_gather.14 = f32[5,1,64,128]{3,2,0,1:T(8,128)S(1)} all-gather(f32[5,1,8,128]{3,2,0,1:T(8,128)S(1)} %psum.30), channel_id=1, replica_groups=mesh['tx'=8,'ty'=4] {'tx'}, dimensions={2}, use_global_device_ids=true | all-gather | bytes 184320 | tf_op jit(solution)/shard_map/all_gather | solution.py:87
  166.2 0.2 pad_maximum_fusion.10
  166.4 0.1 collective-permute-start.6
  166.5 2.0 %collective-permute-start.7 = (f32[2,5,3,1,10,128]{5,3,2,1,4,0:T(1,128)S(1)}, f32[2,5,3,1,10,128]{5,3,2,1,4,0:T(1,128)S(1)}, u32[]{:S(2)}, u32[]{:S(2)}) collective-permute-start(f32[2,5,3,1,10,128]{5,3,2,1,4,0:T(1,128)S(1)} %get-tuple-element.23), channel_id=1, source_target_pairs={{0,1},{1,2},{2,3},{3,0},{4,5},{5,6},{6,7},{7,4},{8,9},{9,10},{10,1... | collective-permute-start | bytes 460808 | tf_op jit(solution)/shard_map/ppermute | solution.py:15
  168.6 0.1 multiply_reduce_fusion.1
  168.7 0.1 bitcast_add_fusion
  168.8 0.0 copy-start.4
  168.8 4.4 %collective-permute-done.6 = f32[2,5,3,1,10,128]{5,3,2,1,4,0:T(1,128)S(1)} collective-permute-done((f32[2,5,3,1,10,128]{5,3,2,1,4,0:T(1,128)S(1)}, f32[2,5,3,1,10,128]{5,3,2,1,4,0:T(1,128)S(1)}, u32[]{:S(2)}, u32[]{:S(2)}) %collective-permute-start.6) | collective-permute-done | bytes 153632 | tf_op jit(solution)/shard_map/ppermute | solution.py:18
  173.3 2.8 %collective-permute-done.7 = f32[2,5,3,1,10,128]{5,3,2,1,4,0:T(1,128)S(1)} collective-permute-done((f32[2,5,3,1,10,128]{5,3,2,1,4,0:T(1,128)S(1)}, f32[2,5,3,1,10,128]{5,3,2,1,4,0:T(1,128)S(1)}, u32[]{:S(2)}, u32[]{:S(2)}) %collective-permute-start.7) | collective-permute-done | bytes 153632 | tf_op jit(solution)/shard_map/ppermute | solution.py:15
  176.1 0.1 multiply_reduce_fusion.5
  176.2 0.1 broadcast_select_fusion.1
  176.3 0.2 broadcast_select_fusion.3
  176.5 0.3 fusion
  176.8 1.8 fusion.4
  (50 shorter events, 0.4 us)
Async XLA Ops:
  0.0 1.3 copy-start
  3.3 0.9 copy-start.1
  4.4 4.3 %copy-start.8 = (s32[40,4]{0,1:T(4,128)S(1)}, s32[40,4]{0,1:T(4,128)}, u32[]{:S(2)}) copy-start(s32[40,4]{0,1:T(4,128)} %param.7) | copy-start | bytes 1924
  5.4 75.9 %collective-permute-start.1 = (f32[2,5,3,16,1,128]{5,3,2,1,4,0:T(8,128)}, f32[2,5,3,16,1,128]{5,3,2,1,4,0:T(8,128)}, u32[]{:S(2)}, u32[]{:S(2)}) collective-permute-start(f32[2,5,3,16,1,128]{5,3,2,1,4,0:T(8,128)} %get-tuple-element.32), channel_id=1, source_target_pairs={{0,4},{4,8},{8,12},{12,16},{16,20},{20,24},{24,28},{28,0},{1,5},{5... | collective-permute-start | bytes 737288 | tf_op jit(solution)/shard_map/ppermute | solution.py:15
  5.9 75.5 %collective-permute-start = (f32[2,5,3,16,1,128]{5,3,2,1,4,0:T(8,128)}, f32[2,5,3,16,1,128]{5,3,2,1,4,0:T(8,128)}, u32[]{:S(2)}, u32[]{:S(2)}) collective-permute-start(f32[2,5,3,16,1,128]{5,3,2,1,4,0:T(8,128)} %get-tuple-element.33), channel_id=1, source_target_pairs={{4,0},{8,4},{12,8},{16,12},{20,16},{24,20},{28,24},{0,28},{5,1},{9... | collective-permute-start | bytes 737288 | tf_op jit(solution)/shard_map/ppermute | solution.py:18
  81.3 5.4 %copy-start.10 = (f32[3]{0:T(128)S(1)}, f32[3]{0:T(128)}, u32[]{:S(2)}) copy-start(f32[3]{0:T(128)} %neg.18) | copy-start | bytes 40
  82.7 6.8 %collective-permute-start.2 = (f32[2,5,3,1,10,128]{5,3,2,1,4,0:T(1,128)S(1)}, f32[2,5,3,1,10,128]{5,3,2,1,4,0:T(1,128)S(1)}, u32[]{:S(2)}, u32[]{:S(2)}) collective-permute-start(f32[2,5,3,1,10,128]{5,3,2,1,4,0:T(1,128)S(1)} %get-tuple-element.24), channel_id=1, source_target_pairs={{1,0},{2,1},{3,2},{0,3},{5,4},{6,5},{7,6},{4,7},{9,8},{10,9},{11,1... | collective-permute-start | bytes 460808 | tf_op jit(solution)/shard_map/ppermute | solution.py:18
  82.8 9.5 %collective-permute-start.3 = (f32[2,5,3,1,10,128]{5,3,2,1,4,0:T(1,128)S(1)}, f32[2,5,3,1,10,128]{5,3,2,1,4,0:T(1,128)S(1)}, u32[]{:S(2)}, u32[]{:S(2)}) collective-permute-start(f32[2,5,3,1,10,128]{5,3,2,1,4,0:T(1,128)S(1)} %get-tuple-element.25), channel_id=1, source_target_pairs={{0,1},{1,2},{2,3},{3,0},{4,5},{5,6},{6,7},{7,4},{8,9},{9,10},{10,1... | collective-permute-start | bytes 460808 | tf_op jit(solution)/shard_map/ppermute | solution.py:15
  86.7 5.9 %copy-start.9 = (f32[3]{0:T(128)S(1)}, f32[3]{0:T(128)}, u32[]{:S(2)}) copy-start(f32[3]{0:T(128)} %neg.19) | copy-start | bytes 40
  88.7 4.3 %copy-start.2 = (f32[5,3,16,8,128]{4,3,2,1,0:T(8,128)S(1)}, f32[5,3,16,8,128]{4,3,2,1,0:T(8,128)}, u32[]{:S(2)}) copy-start(f32[5,3,16,8,128]{4,3,2,1,0:T(8,128)} %copy-done.1) | copy-start | bytes 2949124
  88.8 4.3 %copy-start.7 = (f32[5,128,128]{2,1,0:T(8,128)S(1)}, f32[5,128,128]{2,1,0:T(8,128)}, u32[]{:S(2)}) copy-start(f32[5,128,128]{2,1,0:T(8,128)} %param.6) | copy-start | bytes 983044
  94.8 0.9 copy-start.3
  134.7 31.5 %collective-permute-start.5 = (f32[2,5,3,16,1,128]{5,3,2,1,4,0:T(8,128)}, f32[2,5,3,16,1,128]{5,3,2,1,4,0:T(8,128)S(1)}, u32[]{:S(2)}, u32[]{:S(2)}) collective-permute-start(f32[2,5,3,16,1,128]{5,3,2,1,4,0:T(8,128)} %get-tuple-element.28), channel_id=1, source_target_pairs={{0,4},{4,8},{8,12},{12,16},{16,20},{20,24},{24,28},{28,0},{1,5},{5... | collective-permute-start | bytes 737288 | tf_op jit(solution)/shard_map/ppermute | solution.py:15
  134.7 31.5 %collective-permute-start.4 = (f32[2,5,3,16,1,128]{5,3,2,1,4,0:T(8,128)}, f32[2,5,3,16,1,128]{5,3,2,1,4,0:T(8,128)S(1)}, u32[]{:S(2)}, u32[]{:S(2)}) collective-permute-start(f32[2,5,3,16,1,128]{5,3,2,1,4,0:T(8,128)} %get-tuple-element.29), channel_id=1, source_target_pairs={{4,0},{8,4},{12,8},{16,12},{20,16},{24,20},{28,24},{0,28},{5,1},{9... | collective-permute-start | bytes 737288 | tf_op jit(solution)/shard_map/ppermute | solution.py:18
  166.4 10.1 %copy-start.5 = (f32[5,3,16,8,128]{4,2,1,0,3:T(8,128)S(1)}, f32[5,3,16,8,128]{4,2,1,0,3:T(8,128)}, u32[]{:S(2)}) copy-start(f32[5,3,16,8,128]{4,2,1,0,3:T(8,128)} %get-tuple-element.26) | copy-start | bytes 2949124
  166.4 6.8 %collective-permute-start.6 = (f32[2,5,3,1,10,128]{5,3,2,1,4,0:T(1,128)S(1)}, f32[2,5,3,1,10,128]{5,3,2,1,4,0:T(1,128)S(1)}, u32[]{:S(2)}, u32[]{:S(2)}) collective-permute-start(f32[2,5,3,1,10,128]{5,3,2,1,4,0:T(1,128)S(1)} %get-tuple-element.22), channel_id=1, source_target_pairs={{1,0},{2,1},{3,2},{0,3},{5,4},{6,5},{7,6},{4,7},{9,8},{10,9},{11,1... | collective-permute-start | bytes 460808 | tf_op jit(solution)/shard_map/ppermute | solution.py:18
  166.5 9.6 %collective-permute-start.7 = (f32[2,5,3,1,10,128]{5,3,2,1,4,0:T(1,128)S(1)}, f32[2,5,3,1,10,128]{5,3,2,1,4,0:T(1,128)S(1)}, u32[]{:S(2)}, u32[]{:S(2)}) collective-permute-start(f32[2,5,3,1,10,128]{5,3,2,1,4,0:T(1,128)S(1)} %get-tuple-element.23), channel_id=1, source_target_pairs={{0,1},{1,2},{2,3},{3,0},{4,5},{5,6},{6,7},{7,4},{8,9},{9,10},{10,1... | collective-permute-start | bytes 460808 | tf_op jit(solution)/shard_map/ppermute | solution.py:15
  168.8 8.0 %copy-start.4 = (f32[5,3,16,8,128]{4,3,2,1,0:T(8,128)S(1)}, f32[5,3,16,8,128]{4,3,2,1,0:T(8,128)}, u32[]{:S(2)}) copy-start(f32[5,3,16,8,128]{4,3,2,1,0:T(8,128)} %copy-done.3) | copy-start | bytes 2949124
  168.8 8.0 %copy-start.6 = (f32[1,5,3,16,8,128]{5,4,3,2,1,0:T(8,128)S(1)}, f32[1,5,3,16,8,128]{5,4,3,2,1,0:T(8,128)}, u32[]{:S(2)}) copy-start(f32[1,5,3,16,8,128]{5,4,3,2,1,0:T(8,128)} %copy.252) | copy-start | bytes 2949124
where the time goes:
time: 179 us
  blocking collectives  129 us (72%)
  local copies, waits for them, and re-layouts  11.1 us (6%)
  waiting for transfers between devices  10.7 us (6%)
  starting transfers between devices  10.1 us (6%)
  other arithmetic  9.29 us (5%)
  between operations  4.59 us (3%)
  matrix products  3.63 us (2%)
    psum x4, blocking collectives, broadcast(): return lax.psum(block, axis)  84 us
    all_gather x2, blocking collectives, on_device(): east_whole = lax.all_gather(east_beside, 'ty', axis=2, tiled=True)  26.9 us
    all_gather x2, blocking collectives, on_device(): north_whole = lax.all_gather(north_below, 'tx', axis=2, tiled=True)  18.2 us
    ppermute x4, starting transfers between devices, with_halo(): lax.ppermute(lax.slice_in_dim(block, 0, width, axis=dim), axis, backward)  5.73 us
    ppermute x4, waiting for transfers between devices, with_halo(): lax.ppermute(lax.slice_in_dim(block, block.shape[dim] - width, None, axis...  5.56 us
    ppermute x4, waiting for transfers between devices, with_halo(): lax.ppermute(lax.slice_in_dim(block, 0, width, axis=dim), axis, backward)  5.12 us
    ppermute x4, starting transfers between devices, with_halo(): lax.ppermute(lax.slice_in_dim(block, block.shape[dim] - width, None, axis...  4.4 us
    dot_general x2, matrix products, on_device(): jnp.einsum('slm,skyxl->skyxm', vertical_inverse, adjoint, precision=lax.P...  3.63 us
  transfers between devices with their start and end apart: 8, of which 4 were waited for; matrix products, arithmetic and copies ran while one was open for 5% of the time, Pallas kernels for 0%

commit v1 on v0

v1 whole, which is shorter than its diff:
```python
import functools

import jax
import jax.numpy as jnp
from jax import lax
from jax.experimental import pallas as pl
from jax.experimental.pallas import tpu as pltpu
from jax.sharding import PartitionSpec as P

STEPS = 2
EAST, WEST, NORTH, SOUTH = range(4)


def kernel(
    species, slots, cells_y, cells_x, cols, rows,
    adj_ref, courant_ref, inverse_ref, links_ref, out_ref,
    mid, mixed, sent, received, to_turn_n, to_turn_e, from_turn_e, from_turn_n,
    send_sems, recv_sems, turn_send, turn_recv,
):
    ratio = cells_y // cells_x
    tile_count = cols * rows
    col = lax.axis_index("tx")
    row = lax.axis_index("ty")
    at_east, at_west = col == cols - 1, col == 0
    at_north, at_south = row == rows - 1, row == 0
    seam = (at_east, at_west, at_north, at_south)
    far_seam = (at_west, at_east, at_south, at_north)
    east, west = lax.rem(col + 1, cols), lax.rem(col + cols - 1, cols)
    north, south = lax.rem(row + 1, rows), lax.rem(row + rows - 1, rows)
    targets = ({"tx": east}, {"tx": west}, {"ty": north}, {"ty": south})
    turn_row = lax.div(col * cells_x, cells_y)
    turn_part = lax.rem(col, ratio)
    north_turns = {"tx": cols - 1, "ty": turn_row}
    north_remote = at_north & jnp.logical_not(at_east)
    east_turns = [{"tx": row * ratio + j, "ty": rows - 1} for j in range(ratio)]
    corner = at_east & at_north
    east_remote = [
        at_east & jnp.logical_not(at_north) if j == ratio - 1 else at_east for j in range(ratio)
    ]

    barrier = pltpu.get_barrier_semaphore()

    def greet(device):
        pl.semaphore_signal(
            barrier, inc=1, device_id=device, device_id_type=pl.DeviceIdType.MESH
        )

    for device in targets:
        greet(device)

    @pl.when(north_remote)
    def _():
        greet(north_turns)

    for j in range(ratio):

        @pl.when(east_remote[j])
        def _(j=j):
            greet(east_turns[j])

    def read_link(index, faces):
        turned = links_ref[index, 3] == 2
        source = lax.div(links_ref[index, 0], tile_count)
        target = lax.div(links_ref[index, 1], tile_count)
        return jnp.where(turned, source, faces[0]), jnp.where(turned, target, faces[1])

    zero = jnp.int32(0)
    face_y, face_z = lax.fori_loop(0, links_ref.shape[0], read_link, (zero, zero))
    face_x = jnp.clip(slots - face_y - face_z, 0, slots - 1)
    face_y = jnp.clip(face_y, 0, slots - 1)
    face_z = jnp.clip(face_z, 0, slots - 1)

    def weight(face, slot, value):
        return jnp.where(face == slot, jnp.float32(value), jnp.float32(0.0))

    first_col = pl.ds(0, cells_y, stride=cells_x)
    last_col = pl.ds(cells_x - 1, cells_y, stride=cells_x)
    first_row = pl.ds(0, cells_x)
    last_row = pl.ds((cells_y - 1) * cells_x, cells_x)
    strips = (last_col, first_col, last_row, first_row)
    seam_faces = (face_x, face_y, face_x, face_z)

    def outgoing(step, side):
        return sent[step][side]

    def incoming(step, side):
        return received[step][side]

    def halo_copy(step, side, short):
        source, target = outgoing(step, side), incoming(step, side)
        if short:
            source, target = source.at[pl.ds(0, species)], target.at[pl.ds(0, species)]
        return pltpu.make_async_remote_copy(
            src_ref=source,
            dst_ref=target,
            send_sem=send_sems.at[step, side],
            recv_sem=recv_sems.at[step, side],
            device_id=targets[side],
            device_id_type=pl.DeviceIdType.MESH,
        )

    def north_copy(step, part):
        return pltpu.make_async_remote_copy(
            src_ref=to_turn_n[step],
            dst_ref=from_turn_e[step][part],
            send_sem=turn_send.at[step, ratio],
            recv_sem=turn_recv.at[step, part],
            device_id=north_turns,
            device_id_type=pl.DeviceIdType.MESH,
        )

    def east_copy(step, part):
        return pltpu.make_async_remote_copy(
            src_ref=to_turn_e[step][part],
            dst_ref=from_turn_n[step],
            send_sem=turn_send.at[step, part],
            recv_sem=turn_recv.at[step, ratio],
            device_id=east_turns[part],
            device_id_type=pl.DeviceIdType.MESH,
        )

    def either(condition, act):
        pl.when(condition)(functools.partial(act, True))
        pl.when(jnp.logical_not(condition))(functools.partial(act, False))

    lane_x = lax.broadcasted_iota(jnp.int32, (cells_y, cells_x, mixed.shape[-1]), 1)

    for step in range(STEPS):
        source = adj_ref if step == 0 else mid
        target = mid if step < STEPS - 1 else out_ref

        @pl.loop(0, species)
        def _(s):
            base = s * slots
            values = source[pl.ds(base, slots)].reshape(slots * cells_y * cells_x, -1)
            high = values.astype(jnp.bfloat16)
            low = (values - high.astype(jnp.float32)).astype(jnp.bfloat16)
            inverse = inverse_ref[s]
            inverse_high = inverse.astype(jnp.bfloat16)
            inverse_low = (inverse - inverse_high.astype(jnp.float32)).astype(jnp.bfloat16)
            both = jnp.concatenate([inverse_high, inverse_low], axis=1)
            product = jnp.dot(
                jnp.concatenate([high, low], axis=1),
                jnp.concatenate([both, both], axis=0),
                preferred_element_type=jnp.float32,
            )
            levels = inverse.shape[-1]
            product = product[:, :levels] + product[:, levels:]
            mixed[pl.ds(base, slots)] = product.reshape(slots, cells_y * cells_x, levels)
            for k in range(slots):
                for side in range(4):
                    strip = strips[side]
                    flux = courant_ref[side // 2, k, strip, :] * mixed[base + k, strip, :]
                    outgoing(step, side)[base + k] = flux

        for side in range(4):

            @pl.when(seam[side])
            def _(side=side):
                strip, face = strips[side], seam_faces[side]
                factor = courant_ref[side // 2, face, strip, :]
                for s in range(species):
                    outgoing(step, side)[s] = factor * mixed[s * slots + face, strip, :]

        @pl.when(at_north)
        def _():
            factor = courant_ref[1, face_y, last_row, :]
            for s in range(species):
                to_turn_n[step][s] = factor * mixed[s * slots + face_y, last_row, :]

        @pl.when(at_east)
        def _():
            for j in range(ratio):
                strip = pl.ds(j * cells_x * cells_x + cells_x - 1, cells_x, stride=cells_x)
                factor = courant_ref[0, face_z, strip, :]
                for s in range(species):
                    to_turn_e[step][j][s] = factor * mixed[s * slots + face_z, strip, :]

        if step == 0:
            peers = 4 + sum(c.astype(jnp.int32) for c in [north_remote, *east_remote])
            pl.semaphore_wait(barrier, peers)

        for j in range(ratio):

            @pl.when(north_remote & (turn_part == j))
            def _(j=j):
                north_copy(step, j).start()

            @pl.when(east_remote[j])
            def _(j=j):
                east_copy(step, j).start()

        for side in range(4):
            either(seam[side], lambda short, side=side: halo_copy(step, side, short).start())

        @pl.when(corner)
        def _():
            from_turn_e[step][ratio - 1][...] = to_turn_n[step][...]
            from_turn_n[step][...] = to_turn_e[step][ratio - 1][...]

        @pl.loop(0, species)
        def _(s):
            for k in range(slots):
                here = mixed[s * slots + k].reshape(cells_y, cells_x, -1)
                along_x = 0.5 * courant_ref[0, k].reshape(here.shape) * here
                along_y = 0.5 * courant_ref[1, k].reshape(here.shape) * here
                ahead = jnp.where(
                    lane_x == cells_x - 1, 0.0, pltpu.roll(along_x, cells_x - 1, 1)
                )
                behind = jnp.where(lane_x == 0, 0.0, pltpu.roll(along_x, 1, 1))
                nothing = jnp.zeros_like(along_y[:1])
                above = jnp.concatenate([along_y[1:], nothing], axis=0)
                below = jnp.concatenate([nothing, along_y[:-1]], axis=0)
                result = here + (ahead - behind) + (above - below)
                target[s * slots + k] = result.reshape(cells_y * cells_x, -1)

        for side in range(4):
            either(
                far_seam[side], lambda short, side=side: halo_copy(step, side, short).wait_recv()
            )

        @pl.when(at_east)
        def _():
            for j in range(ratio):
                if j < ratio - 1:
                    north_copy(step, j).wait_recv()
                else:

                    @pl.when(east_remote[j])
                    def _():
                        north_copy(step, ratio - 1).wait_recv()

        @pl.when(north_remote)
        def _():
            east_copy(step, 0).wait_recv()

        boundary = (first_col, last_col, first_row, last_row)
        sign = (-0.5, 0.5, -0.5, 0.5)
        filled = (face_y, face_x, face_z, face_x)
        for side in range(4):
            strip = boundary[side]

            @pl.when(jnp.logical_not(far_seam[side]))
            def _(side=side, strip=strip):
                @pl.loop(0, species)
                def _(s):
                    for k in range(slots):
                        index = s * slots + k
                        ghost = incoming(step, side)[index]
                        target[index, strip, :] = target[index, strip, :] + sign[side] * ghost

            @pl.when(far_seam[side])
            def _(side=side, strip=strip):
                @pl.loop(0, species)
                def _(s):
                    ghost = incoming(step, side)[s]
                    for k in range(slots):
                        index = s * slots + k
                        value = target[index, strip, :]
                        value = value + weight(filled[side], k, sign[side]) * ghost
                        if side == WEST:
                            turned = jnp.concatenate(
                                [from_turn_e[step][j][s] for j in range(ratio)], axis=0
                            )
                            value = value - weight(face_z, k, 0.5) * turned
                        if side == SOUTH:
                            value = value - weight(face_y, k, 0.5) * from_turn_n[step][s]
                        target[index, strip, :] = value

    for step in range(STEPS):
        for side in range(4):
            either(seam[side], lambda short, side=side: halo_copy(step, side, short).wait_send())

        for j in range(ratio):

            @pl.when(north_remote & (turn_part == j))
            def _(j=j):
                north_copy(step, j).wait_send()

            @pl.when(east_remote[j])
            def _(j=j):
                east_copy(step, j).wait_send()


def on_device(adjoint_in, courant, vertical_inverse, links):
    cols, rows = lax.axis_size("tx"), lax.axis_size("ty")
    species, slots, cells_y, cells_x, levels = adjoint_in.shape
    ratio = cells_y // cells_x
    planes, cells = species * slots, cells_y * cells_x
    vmem = pl.BlockSpec(memory_space=pltpu.VMEM)

    def buffer(*shape):
        return pltpu.VMEM(shape + (levels,), jnp.float32)

    halo = [buffer(planes, cells_y)] * 2 + [buffer(planes, cells_x)] * 2
    turn = buffer(species, cells_x)
    result = pl.pallas_call(
        functools.partial(kernel, species, slots, cells_y, cells_x, cols, rows),
        out_shape=jax.ShapeDtypeStruct((planes, cells, levels), jnp.float32),
        in_specs=[vmem, vmem, vmem, pl.BlockSpec(memory_space=pltpu.SMEM)],
        out_specs=vmem,
        scratch_shapes=[
            buffer(planes, cells),
            buffer(planes, cells),
            [halo] * STEPS,
            [halo] * STEPS,
            [turn] * STEPS,
            [[turn] * ratio] * STEPS,
            [[turn] * ratio] * STEPS,
            [turn] * STEPS,
            pltpu.SemaphoreType.DMA((STEPS, 4)),
            pltpu.SemaphoreType.DMA((STEPS, 4)),
            pltpu.SemaphoreType.DMA((STEPS, ratio + 1)),
            pltpu.SemaphoreType.DMA((STEPS, ratio + 1)),
        ],
        compiler_params=pltpu.CompilerParams(
            collective_id=0, has_side_effects=True, vmem_limit_bytes=32 * 1024 * 1024
        ),
    )(
        adjoint_in.reshape(planes, cells, levels),
        courant.reshape(2, slots, cells, levels),
        vertical_inverse,
        links,
    )
    return result.reshape(adjoint_in.shape)


def solution(mesh):
    placed = (P(None, None, "ty", "tx", None), P(None, None, "ty", "tx", None), P(), P())
    return jax.shard_map(
        on_device,
        mesh=mesh,
        in_specs=placed,
        out_specs=P(None, None, "ty", "tx", None),
        check_vma=False,
    )
```

time: 179 us -> 22.4 us (0.13)
  blocking collectives: 129 us -> 0 us
  Pallas kernels: 0 us -> 17.3 us
  waiting for transfers between devices: 10.7 us -> 0 us
  starting transfers between devices: 10.1 us -> 0 us
  other arithmetic: 9.29 us -> 0 us
  local copies, waits for them, and re-layouts: 11.1 us -> 4.89 us
  between operations: 4.59 us -> 0.01 us
  matrix products: 3.63 us -> 0 us
    psum x4 -> x0, blocking collectives: 84 us -> none  [broadcast(): return lax.psum(block, axis)]
    all_gather x4 -> x0, blocking collectives: 45.1 us -> none  [the longest x2 26.9 us: on_device(): east_whole = lax.all_gather(east_beside, 'ty', axis=2, tiled=True)]
    pallas_call x0 -> x1, Pallas kernels: none -> 17.3 us  [on_device(): pl.pallas_call(functools.partial(kernel, species, slots, cells_y, cells_x...]
    ppermute x8 -> x0, waiting for transfers between devices: 10.7 us -> none  [the longest x4 5.56 us: with_halo(): lax.ppermute(lax.slice_in_dim(block, block.shape[dim] - width, None, axis...]
    ppermute x8 -> x0, starting transfers between devices: 10.1 us -> none  [the longest x4 5.73 us: with_halo(): lax.ppermute(lax.slice_in_dim(block, 0, width, axis=dim), axis, backward)]
    slice x16 -> x0, local copies, waits for them, and re-layouts: 4.45 us -> none  [the longest x1 2.5 us: on_device(): fluxes[0]]
    dot_general x2 -> x0, matrix products: 3.63 us -> none  [on_device(): jnp.einsum('slm,skyxl->skyxm', vertical_inverse, adjoint, precision=lax.P...]
    select_n x12 -> x0, other arithmetic: 2.56 us -> none  [the longest x2 1.01 us: on_device(): jnp.where(at_east, mix_slots(x_table, halo_east) + rotated_east, halo_east)]
  transfers between devices with their start and end apart: 8 -> 0, of which waited for: 4 -> 0; matrix products, arithmetic and copies ran while one was open for 5% -> 0% of each run, Pallas kernels for 0% -> 0%
where the time goes in v1:
time: 22.4 us; the launch traced here: 22.2 us
  Pallas kernels  17.3 us (77%)
  local copies, waits for them, and re-layouts  4.89 us (22%)
    pallas_call x1, Pallas kernels, on_device(): pl.pallas_call(functools.partial(kernel, species, slots, cells_y, cells_x...  17.3 us
    unnamed x10, local copies, waits for them, and re-layouts  4.89 us

profile of v1, /device:TPU:0, one launch (start us, length us, event | category | flops | bytes accessed | tf_op | source)
XLA Modules:
  0.0 22.2 jit_solution(14126951391106493057)
XLA Ops:
  0.0 0.0 copy-start.3
  0.0 0.7 %copy-done.3 = s32[40,4]{0,1:T(4,128)S(1)} copy-done((s32[40,4]{0,1:T(4,128)S(1)}, s32[40,4]{0,1:T(4,128)}, u32[]{:S(2)}) %copy-start.3) | copy-done | bytes 664
  0.7 0.1 copy.5.links_ref
  0.8 0.0 copy-start
  0.8 1.2 %copy-done = f32[5,3,16,8,128]{4,3,2,1,0:T(8,128)S(1)} copy-done((f32[5,3,16,8,128]{4,3,2,1,0:T(8,128)S(1)}, f32[5,3,16,8,128]{4,3,2,1,0:T(8,128)}, u32[]{:S(2)}) %copy-start) | copy-done | bytes 983064
  2.0 0.0 copy-start.1
  2.0 1.0 %copy-done.1 = f32[2,3,16,8,128]{4,3,2,1,0:T(8,128)S(1)} copy-done((f32[2,3,16,8,128]{4,3,2,1,0:T(8,128)S(1)}, f32[2,3,16,8,128]{4,3,2,1,0:T(8,128)}, u32[]{:S(2)}) %copy-start.1) | copy-done | bytes 393240
  3.0 0.0 copy-start.2
  3.0 1.0 %copy-done.2 = f32[5,128,128]{2,1,0:T(8,128)S(1)} copy-done((f32[5,128,128]{2,1,0:T(8,128)S(1)}, f32[5,128,128]{2,1,0:T(8,128)}, u32[]{:S(2)}) %copy-start.2) | copy-done | bytes 327704
  3.9 17.3 %shard_map.46 = f32[15,128,128]{2,1,0:T(8,128)S(1)} custom-call(f32[15,128,128]{2,1,0:T(8,128)S(1)} %bitcast.4, f32[2,3,128,128]{3,2,1,0:T(8,128)S(1)} %bitcast.5, f32[5,128,128]{2,1,0:T(8,128)S(1)} %copy-done.2, s32[40,4]{1,0:T(8,128)S(1)} %copy.5.links_ref), custom_call_target="tpu_custom_call" | custom-call | tf_op jit(solution)/shard_map/pallas_call | solution.py:297
  21.2 0.9 %copy.7 = f32[5,3,16,8,128]{4,3,2,1,0:T(8,128)} copy(f32[5,3,16,8,128]{4,3,2,1,0:T(8,128)S(1)} %bitcast.3) | data formatting | bytes 1966080
Async XLA Ops:
  0.0 0.7 %copy-start.3 = (s32[40,4]{0,1:T(4,128)S(1)}, s32[40,4]{0,1:T(4,128)}, u32[]{:S(2)}) copy-start(s32[40,4]{0,1:T(4,128)} %param.7) | copy-start | bytes 1924
  0.8 1.2 %copy-start = (f32[5,3,16,8,128]{4,3,2,1,0:T(8,128)S(1)}, f32[5,3,16,8,128]{4,3,2,1,0:T(8,128)}, u32[]{:S(2)}) copy-start(f32[5,3,16,8,128]{4,3,2,1,0:T(8,128)} %param.4) | copy-start | bytes 2949124
  2.0 1.0 %copy-start.1 = (f32[2,3,16,8,128]{4,3,2,1,0:T(8,128)S(1)}, f32[2,3,16,8,128]{4,3,2,1,0:T(8,128)}, u32[]{:S(2)}) copy-start(f32[2,3,16,8,128]{4,3,2,1,0:T(8,128)} %param.5) | copy-start | bytes 1179652
  3.0 1.0 %copy-start.2 = (f32[5,128,128]{2,1,0:T(8,128)S(1)}, f32[5,128,128]{2,1,0:T(8,128)}, u32[]{:S(2)}) copy-start(f32[5,128,128]{2,1,0:T(8,128)} %inverse_ref.1) | copy-start | bytes 983044

commit v2 on v1

--- a/solution.py
+++ b/solution.py
@@ -13,9 +13,10 @@
 
 def kernel(
     species, slots, cells_y, cells_x, cols, rows,
-    adj_ref, courant_ref, inverse_ref, links_ref, out_ref,
+    adj_hbm, courant_hbm, inverse_hbm, links_hbm, out_ref,
+    adj_ref, courant_ref, inverse_ref, links_ref,
     mid, mixed, sent, received, to_turn_n, to_turn_e, from_turn_e, from_turn_n,
-    send_sems, recv_sems, turn_send, turn_recv,
+    send_sems, recv_sems, turn_send, turn_recv, load_sems,
 ):
     ratio = cells_y // cells_x
     tile_count = cols * rows
@@ -58,14 +59,30 @@
         def _(j=j):
             greet(east_turns[j])
 
-    def read_link(index, faces):
-        turned = links_ref[index, 3] == 2
-        source = lax.div(links_ref[index, 0], tile_count)
-        target = lax.div(links_ref[index, 1], tile_count)
-        return jnp.where(turned, source, faces[0]), jnp.where(turned, target, faces[1])
+    loads = [
+        pltpu.make_async_copy(links_hbm, links_ref, load_sems.at[0]),
+        pltpu.make_async_copy(inverse_hbm, inverse_ref, load_sems.at[1]),
+    ]
+    for s in range(species):
+        planes = pl.ds(s * slots, slots)
+        loads.append(
+            pltpu.make_async_copy(adj_hbm.at[planes], adj_ref.at[planes], load_sems.at[3 + s])
+        )
+    loads.append(pltpu.make_async_copy(courant_hbm, courant_ref, load_sems.at[2]))
+    for load in loads:
+        load.start()
+    loads[0].wait()
+
+    def read_link(index, tiles):
+        turned = links_ref[3, index] == 2
+        return (
+            jnp.where(turned, links_ref[0, index], tiles[0]),
+            jnp.where(turned, links_ref[1, index], tiles[1]),
+        )
 
     zero = jnp.int32(0)
-    face_y, face_z = lax.fori_loop(0, links_ref.shape[0], read_link, (zero, zero))
+    tile_y, tile_z = lax.fori_loop(0, links_ref.shape[1], read_link, (zero, zero))
+    face_y, face_z = lax.div(tile_y, tile_count), lax.div(tile_z, tile_count)
     face_x = jnp.clip(slots - face_y - face_z, 0, slots - 1)
     face_y = jnp.clip(face_y, 0, slots - 1)
     face_z = jnp.clip(face_z, 0, slots - 1)
@@ -129,9 +146,13 @@
         source = adj_ref if step == 0 else mid
         target = mid if step < STEPS - 1 else out_ref
 
-        @pl.loop(0, species)
-        def _(s):
+        if step == 0:
+            loads[1].wait()
+            loads[-1].wait()
+        for s in range(species):
             base = s * slots
+            if step == 0:
+                loads[2 + s].wait()
             values = source[pl.ds(base, slots)].reshape(slots * cells_y * cells_x, -1)
             high = values.astype(jnp.bfloat16)
             low = (values - high.astype(jnp.float32)).astype(jnp.bfloat16)
@@ -198,8 +219,7 @@
             from_turn_e[step][ratio - 1][...] = to_turn_n[step][...]
             from_turn_n[step][...] = to_turn_e[step][ratio - 1][...]
 
-        @pl.loop(0, species)
-        def _(s):
+        for s in range(species):
             for k in range(slots):
                 here = mixed[s * slots + k].reshape(cells_y, cells_x, -1)
                 along_x = 0.5 * courant_ref[0, k].reshape(here.shape) * here
@@ -242,8 +262,7 @@
 
             @pl.when(jnp.logical_not(far_seam[side]))
             def _(side=side, strip=strip):
-                @pl.loop(0, species)
-                def _(s):
+                for s in range(species):
                     for k in range(slots):
                         index = s * slots + k
                         ghost = incoming(step, side)[index]
@@ -251,8 +270,7 @@
 
             @pl.when(far_seam[side])
             def _(side=side, strip=strip):
-                @pl.loop(0, species)
-                def _(s):
+                for s in range(species):
                     ghost = incoming(step, side)[s]
                     for k in range(slots):
                         index = s * slots + k
@@ -287,7 +305,6 @@
     species, slots, cells_y, cells_x, levels = adjoint_in.shape
     ratio = cells_y // cells_x
     planes, cells = species * slots, cells_y * cells_x
-    vmem = pl.BlockSpec(memory_space=pltpu.VMEM)
 
     def buffer(*shape):
         return pltpu.VMEM(shape + (levels,), jnp.float32)
@@ -297,9 +314,13 @@
     result = pl.pallas_call(
         functools.partial(kernel, species, slots, cells_y, cells_x, cols, rows),
         out_shape=jax.ShapeDtypeStruct((planes, cells, levels), jnp.float32),
-        in_specs=[vmem, vmem, vmem, pl.BlockSpec(memory_space=pltpu.SMEM)],
-        out_specs=vmem,
+        in_specs=[pl.BlockSpec(memory_space=pltpu.HBM)] * 4,
+        out_specs=pl.BlockSpec(memory_space=pltpu.VMEM),
         scratch_shapes=[
+            buffer(planes, cells),
+            buffer(2, slots, cells),
+            buffer(species, levels),
+            pltpu.SMEM(links.shape[::-1], jnp.int32),
             buffer(planes, cells),
             buffer(planes, cells),
             [halo] * STEPS,
@@ -312,15 +333,16 @@
             pltpu.SemaphoreType.DMA((STEPS, 4)),
             pltpu.SemaphoreType.DMA((STEPS, ratio + 1)),
             pltpu.SemaphoreType.DMA((STEPS, ratio + 1)),
+            pltpu.SemaphoreType.DMA((species + 3,)),
         ],
         compiler_params=pltpu.CompilerParams(
-            collective_id=0, has_side_effects=True, vmem_limit_bytes=32 * 1024 * 1024
+            collective_id=0, has_side_effects=True, vmem_limit_bytes=56 * 1024 * 1024
         ),
     )(
         adjoint_in.reshape(planes, cells, levels),
         courant.reshape(2, slots, cells, levels),
         vertical_inverse,
-        links,
+        links.T,
     )
     return result.reshape(adjoint_in.shape)
 

time: 22.4 us -> 19.4 us (0.87)
  local copies, waits for them, and re-layouts: 4.89 us -> 2.23 us
  Pallas kernels: 17.3 us -> 17 us
    unnamed x10 -> x1, local copies, waits for them, and re-layouts: 4.89 us -> 2.23 us
    pallas_call x1, Pallas kernels: 17.3 us -> 17 us  [on_device(): pl.pallas_call(functools.partial(kernel, species, slots, cells_y, cells_x...]
where the time goes in v2:
time: 19.4 us; the launch traced here: 19.2 us
  Pallas kernels  17 us (88%)
  local copies, waits for them, and re-layouts  2.23 us (11%)
    pallas_call x1, Pallas kernels, on_device(): pl.pallas_call(functools.partial(kernel, species, slots, cells_y, cells_x...  17 us
    unnamed x1, local copies, waits for them, and re-layouts  2.23 us

profile of v2, /device:TPU:0, one launch (start us, length us, event | category | flops | bytes accessed | tf_op | source)
XLA Modules:
  0.0 19.2 jit_solution(5969800663644779548)
XLA Ops:
  0.0 17.0 %shard_map.46 = f32[15,128,128]{2,1,0:T(8,128)} custom-call(f32[15,128,128]{2,1,0:T(8,128)} %bitcast.5, f32[2,3,128,128]{3,2,1,0:T(8,128)} %bitcast.6, f32[5,128,128]{2,1,0:T(8,128)} %inverse_hbm.1, s32[4,40]{1,0:T(4,128)} %bitcast.7), custom_call_target="tpu_custom_call" | custom-call | tf_op jit(solution)/shard_map/pallas_call | solution.py:314
  17.0 2.2 %copy.6 = f32[5,3,16,8,128]{4,3,2,1,0:T(8,128)} copy(f32[5,3,16,8,128]{4,3,2,1,0:T(8,128)} %bitcast.4) | data formatting | bytes 1966080

commit v3 on v2

--- a/solution.py
+++ b/solution.py
@@ -313,7 +313,7 @@
     turn = buffer(species, cells_x)
     result = pl.pallas_call(
         functools.partial(kernel, species, slots, cells_y, cells_x, cols, rows),
-        out_shape=jax.ShapeDtypeStruct((planes, cells, levels), jnp.float32),
+        out_shape=buffer(planes, cells),
         in_specs=[pl.BlockSpec(memory_space=pltpu.HBM)] * 4,
         out_specs=pl.BlockSpec(memory_space=pltpu.VMEM),
         scratch_shapes=[
@@ -336,7 +336,7 @@
             pltpu.SemaphoreType.DMA((species + 3,)),
         ],
         compiler_params=pltpu.CompilerParams(
-            collective_id=0, has_side_effects=True, vmem_limit_bytes=56 * 1024 * 1024
+            collective_id=0, has_side_effects=True, vmem_limit_bytes=54600 * 1024
         ),
     )(
         adjoint_in.reshape(planes, cells, levels),

time: 19.4 us -> 17.2 us (0.89)
  local copies, waits for them, and re-layouts: 2.23 us -> 0.95 us
  Pallas kernels: 17 us -> 16 us
    unnamed x1, local copies, waits for them, and re-layouts: 2.23 us -> 0.95 us
    pallas_call x1, Pallas kernels: 17 us -> 16 us  [on_device(): pl.pallas_call(functools.partial(kernel, species, slots, cells_y, cells_x...]
where the time goes in v3:
time: 17.2 us; the launch traced here: 17 us
  Pallas kernels  16 us (93%)
  local copies, waits for them, and re-layouts  0.95 us (6%)
    pallas_call x1, Pallas kernels, on_device(): pl.pallas_call(functools.partial(kernel, species, slots, cells_y, cells_x...  16 us
    unnamed x1, local copies, waits for them, and re-layouts  0.95 us

profile of v3, /device:TPU:0, one launch (start us, length us, event | category | flops | bytes accessed | tf_op | source)
XLA Modules:
  0.0 17.0 jit_solution(4924669152151655743)
XLA Ops:
  0.0 16.0 %shard_map.46 = f32[15,128,128]{2,1,0:T(8,128)S(1)} custom-call(f32[15,128,128]{2,1,0:T(8,128)} %bitcast.5, f32[2,3,128,128]{3,2,1,0:T(8,128)} %bitcast.6, f32[5,128,128]{2,1,0:T(8,128)} %inverse_hbm.1, s32[4,40]{1,0:T(4,128)} %bitcast.7), custom_call_target="tpu_custom_call" | custom-call | tf_op jit(solution)/shard_map/pallas_call | solution.py:314
  16.0 0.9 %copy.6 = f32[5,3,16,8,128]{4,3,2,1,0:T(8,128)} copy(f32[5,3,16,8,128]{4,3,2,1,0:T(8,128)S(1)} %bitcast.4) | data formatting | bytes 1966080

commit v4 on v3

--- a/solution.py
+++ b/solution.py
@@ -15,7 +15,7 @@
     species, slots, cells_y, cells_x, cols, rows,
     adj_hbm, courant_hbm, inverse_hbm, links_hbm, out_ref,
     adj_ref, courant_ref, inverse_ref, links_ref,
-    mid, mixed, sent, received, to_turn_n, to_turn_e, from_turn_e, from_turn_n,
+    edges, mixed, sent, received, to_turn_n, to_turn_e, from_turn_e, from_turn_n,
     send_sems, recv_sems, turn_send, turn_recv, load_sems,
 ):
     ratio = cells_y // cells_x
@@ -68,8 +68,8 @@
         loads.append(
             pltpu.make_async_copy(adj_hbm.at[planes], adj_ref.at[planes], load_sems.at[3 + s])
         )
-    loads.append(pltpu.make_async_copy(courant_hbm, courant_ref, load_sems.at[2]))
-    for load in loads:
+    courant_load = pltpu.make_async_copy(courant_hbm, courant_ref, load_sems.at[2])
+    for load in [*loads[:3], courant_load, *loads[3:]]:
         load.start()
     loads[0].wait()
 
@@ -142,32 +142,46 @@
 
     lane_x = lax.broadcasted_iota(jnp.int32, (cells_y, cells_x, mixed.shape[-1]), 1)
 
+    cells, levels = cells_y * cells_x, mixed.shape[-1]
+    boundary = (first_col, last_col, first_row, last_row)
+    lengths = (cells_y, cells_y, cells_x, cells_x)
+    starts = [slots * sum(lengths[:side]) for side in range(4)]
+
+    def apply(s, values):
+        high = values.astype(jnp.bfloat16)
+        low = (values - high.astype(jnp.float32)).astype(jnp.bfloat16)
+        inverse = inverse_ref[s]
+        inverse_high = inverse.astype(jnp.bfloat16)
+        inverse_low = (inverse - inverse_high.astype(jnp.float32)).astype(jnp.bfloat16)
+        both = jnp.concatenate([inverse_high, inverse_low], axis=1)
+        product = jnp.dot(
+            jnp.concatenate([high, low], axis=1),
+            jnp.concatenate([both, both], axis=0),
+            preferred_element_type=jnp.float32,
+        )
+        return product[:, :levels] + product[:, levels:]
+
     for step in range(STEPS):
-        source = adj_ref if step == 0 else mid
-        target = mid if step < STEPS - 1 else out_ref
+        last = step == STEPS - 1
 
         if step == 0:
             loads[1].wait()
-            loads[-1].wait()
+            courant_load.wait()
         for s in range(species):
             base = s * slots
             if step == 0:
                 loads[2 + s].wait()
-            values = source[pl.ds(base, slots)].reshape(slots * cells_y * cells_x, -1)
-            high = values.astype(jnp.bfloat16)
-            low = (values - high.astype(jnp.float32)).astype(jnp.bfloat16)
-            inverse = inverse_ref[s]
-            inverse_high = inverse.astype(jnp.bfloat16)
-            inverse_low = (inverse - inverse_high.astype(jnp.float32)).astype(jnp.bfloat16)
-            both = jnp.concatenate([inverse_high, inverse_low], axis=1)
-            product = jnp.dot(
-                jnp.concatenate([high, low], axis=1),
-                jnp.concatenate([both, both], axis=0),
-                preferred_element_type=jnp.float32,
-            )
-            levels = inverse.shape[-1]
-            product = product[:, :levels] + product[:, levels:]
-            mixed[pl.ds(base, slots)] = product.reshape(slots, cells_y * cells_x, levels)
+            if step == 0:
+                values = adj_ref[pl.ds(base, slots)].reshape(slots * cells, levels)
+                mixed[pl.ds(base, slots)] = apply(s, values).reshape(slots, cells, levels)
+            else:
+                change = apply(s, edges[s])
+                for side in range(4):
+                    for k in range(slots):
+                        place = starts[side] + k * lengths[side]
+                        part = change[place : place + lengths[side]]
+                        strip = boundary[side]
+                        mixed[base + k, strip, :] = mixed[base + k, strip, :] + part
             for k in range(slots):
                 for side in range(4):
                     strip = strips[side]
@@ -220,6 +234,7 @@
             from_turn_n[step][...] = to_turn_e[step][ratio - 1][...]
 
         for s in range(species):
+            results = []
             for k in range(slots):
                 here = mixed[s * slots + k].reshape(cells_y, cells_x, -1)
                 along_x = 0.5 * courant_ref[0, k].reshape(here.shape) * here
@@ -232,7 +247,12 @@
                 above = jnp.concatenate([along_y[1:], nothing], axis=0)
                 below = jnp.concatenate([nothing, along_y[:-1]], axis=0)
                 result = here + (ahead - behind) + (above - below)
-                target[s * slots + k] = result.reshape(cells_y * cells_x, -1)
+                results.append(result.reshape(cells, levels))
+                if last:
+                    out_ref[s * slots + k] = results[-1]
+            if not last:
+                product = apply(s, jnp.concatenate(results, axis=0))
+                mixed[pl.ds(s * slots, slots)] = product.reshape(slots, cells, levels)
 
         for side in range(4):
             either(
@@ -254,28 +274,30 @@
         def _():
             east_copy(step, 0).wait_recv()
 
-        boundary = (first_col, last_col, first_row, last_row)
         sign = (-0.5, 0.5, -0.5, 0.5)
+        def add(s, k, side, value):
+            if last:
+                index, strip = s * slots + k, boundary[side]
+                out_ref[index, strip, :] = out_ref[index, strip, :] + value
+            else:
+                place = pl.ds(starts[side] + k * lengths[side], lengths[side])
+                edges[s, place, :] = value
+
         filled = (face_y, face_x, face_z, face_x)
         for side in range(4):
-            strip = boundary[side]
-
             @pl.when(jnp.logical_not(far_seam[side]))
-            def _(side=side, strip=strip):
+            def _(side=side):
                 for s in range(species):
                     for k in range(slots):
                         index = s * slots + k
-                        ghost = incoming(step, side)[index]
-                        target[index, strip, :] = target[index, strip, :] + sign[side] * ghost
+                        add(s, k, side, sign[side] * incoming(step, side)[index])
 
             @pl.when(far_seam[side])
-            def _(side=side, strip=strip):
+            def _(side=side):
                 for s in range(species):
                     ghost = incoming(step, side)[s]
                     for k in range(slots):
-                        index = s * slots + k
-                        value = target[index, strip, :]
-                        value = value + weight(filled[side], k, sign[side]) * ghost
+                        value = weight(filled[side], k, sign[side]) * ghost
                         if side == WEST:
                             turned = jnp.concatenate(
                                 [from_turn_e[step][j][s] for j in range(ratio)], axis=0
@@ -283,7 +305,7 @@
                             value = value - weight(face_z, k, 0.5) * turned
                         if side == SOUTH:
                             value = value - weight(face_y, k, 0.5) * from_turn_n[step][s]
-                        target[index, strip, :] = value
+                        add(s, k, side, value)
 
     for step in range(STEPS):
         for side in range(4):
@@ -321,7 +343,7 @@
             buffer(2, slots, cells),
             buffer(species, levels),
             pltpu.SMEM(links.shape[::-1], jnp.int32),
-            buffer(planes, cells),
+            buffer(species, slots * 2 * (cells_y + cells_x)),
             buffer(planes, cells),
             [halo] * STEPS,
             [halo] * STEPS,

time: 17.2 us -> 16.3 us (0.948)
  Pallas kernels: 16 us -> 15.2 us
    pallas_call x1, Pallas kernels: 16 us -> 15.2 us  [on_device(): pl.pallas_call(functools.partial(kernel, species, slots, cells_y, cells_x...]
where the time goes in v4:
time: 16.3 us; the launch traced here: 16.1 us
  Pallas kernels  15.2 us (93%)
  local copies, waits for them, and re-layouts  0.95 us (6%)
    pallas_call x1, Pallas kernels, on_device(): pl.pallas_call(functools.partial(kernel, species, slots, cells_y, cells_x...  15.2 us
    unnamed x1, local copies, waits for them, and re-layouts  0.95 us

profile of v4, /device:TPU:0, one launch (start us, length us, event | category | flops | bytes accessed | tf_op | source)
XLA Modules:
  0.0 16.1 jit_solution(14042836436526565077)
XLA Ops:
  0.0 15.2 %shard_map.46 = f32[15,128,128]{2,1,0:T(8,128)S(1)} custom-call(f32[15,128,128]{2,1,0:T(8,128)} %bitcast.5, f32[2,3,128,128]{3,2,1,0:T(8,128)} %bitcast.6, f32[5,128,128]{2,1,0:T(8,128)} %inverse_hbm.1, s32[4,40]{1,0:T(4,128)} %bitcast.7), custom_call_target="tpu_custom_call" | custom-call | tf_op jit(solution)/shard_map/pallas_call | solution.py:336
  15.2 0.9 %copy.6 = f32[5,3,16,8,128]{4,3,2,1,0:T(8,128)} copy(f32[5,3,16,8,128]{4,3,2,1,0:T(8,128)S(1)} %bitcast.4) | data formatting | bytes 1966080

commit v5 on v4

--- a/solution.py
+++ b/solution.py
@@ -61,7 +61,7 @@
 
     loads = [
         pltpu.make_async_copy(links_hbm, links_ref, load_sems.at[0]),
-        pltpu.make_async_copy(inverse_hbm, inverse_ref, load_sems.at[1]),
+        pltpu.make_async_copy(inverse_hbm.at[0], inverse_ref.at[0], load_sems.at[1]),
     ]
     for s in range(species):
         planes = pl.ds(s * slots, slots)
@@ -69,8 +69,15 @@
             pltpu.make_async_copy(adj_hbm.at[planes], adj_ref.at[planes], load_sems.at[3 + s])
         )
     courant_load = pltpu.make_async_copy(courant_hbm, courant_ref, load_sems.at[2])
-    for load in [*loads[:3], courant_load, *loads[3:]]:
+    inverse_loads = loads[1:2] + [
+        pltpu.make_async_copy(inverse_hbm.at[s], inverse_ref.at[s], load_sems.at[2 + species + s])
+        for s in range(1, species)
+    ]
+    for load in [*loads[:3], courant_load]:
         load.start()
+    for s in range(1, species):
+        inverse_loads[s].start()
+        loads[2 + s].start()
     loads[0].wait()
 
     def read_link(index, tiles):
@@ -165,11 +172,11 @@
         last = step == STEPS - 1
 
         if step == 0:
-            loads[1].wait()
             courant_load.wait()
         for s in range(species):
             base = s * slots
             if step == 0:
+                inverse_loads[s].wait()
                 loads[2 + s].wait()
             if step == 0:
                 values = adj_ref[pl.ds(base, slots)].reshape(slots * cells, levels)
@@ -355,7 +362,7 @@
             pltpu.SemaphoreType.DMA((STEPS, 4)),
             pltpu.SemaphoreType.DMA((STEPS, ratio + 1)),
             pltpu.SemaphoreType.DMA((STEPS, ratio + 1)),
-            pltpu.SemaphoreType.DMA((species + 3,)),
+            pltpu.SemaphoreType.DMA((2 * species + 2,)),
         ],
         compiler_params=pltpu.CompilerParams(
             collective_id=0, has_side_effects=True, vmem_limit_bytes=54600 * 1024

time: 16.3 us -> 16.3 us (level)
  no operation moved by 1% of the time
where the time goes in v5:
time: 16.3 us; the launch traced here: 16.2 us
  Pallas kernels  15.2 us (93%)
  local copies, waits for them, and re-layouts  0.95 us (6%)
    pallas_call x1, Pallas kernels, on_device(): pl.pallas_call(functools.partial(kernel, species, slots, cells_y, cells_x...  15.2 us
    unnamed x1, local copies, waits for them, and re-layouts  0.95 us

profile of v5, /device:TPU:0, one launch (start us, length us, event | category | flops | bytes accessed | tf_op | source)
XLA Modules:
  0.0 16.2 jit_solution(16469807726078104501)
XLA Ops:
  0.0 15.2 %shard_map.46 = f32[15,128,128]{2,1,0:T(8,128)S(1)} custom-call(f32[15,128,128]{2,1,0:T(8,128)} %bitcast.5, f32[2,3,128,128]{3,2,1,0:T(8,128)} %bitcast.6, f32[5,128,128]{2,1,0:T(8,128)} %inverse_hbm.1, s32[4,40]{1,0:T(4,128)} %bitcast.7), custom_call_target="tpu_custom_call" | custom-call | tf_op jit(solution)/shard_map/pallas_call | solution.py:343
  15.2 0.9 %copy.6 = f32[5,3,16,8,128]{4,3,2,1,0:T(8,128)} copy(f32[5,3,16,8,128]{4,3,2,1,0:T(8,128)S(1)} %bitcast.4) | data formatting | bytes 1966080
